TPU v7x, 32 devices: a whole 2x2x4 slice. The times are simulated.
32 devices in a mesh: seq: 8 (over z, core), kvh: 2 (over x), batch: 2 (over y).
Axes of the slice: x: 2, y: 2, z: 4, core: 2. Of those that a mesh axis runs over, the one named last changes fastest.
Arguments:
- query: bfloat16 [2048, 1280], P(('batch', 'seq'), 'kvh'), parts along dimension 0, may hold values from -33.3 to 33.3
- self_keys: bfloat16 [2048, 256], P(('batch', 'seq'), 'kvh'), parts along dimension 0, may hold values from -6.4 to 6.4
- self_values: bfloat16 [2048, 256], P(('batch', 'seq'), 'kvh'), parts along dimension 0, may hold values from -6 to 6
- cache_keys: bfloat16 [8192, 256], P(('batch', 'seq'), 'kvh'), parts along dimension 0, may hold values from -6.375 to 6.375
- cache_values: bfloat16 [8192, 256], P(('batch', 'seq'), 'kvh'), parts along dimension 0, may hold values from -6 to 6
- cache_pos: int32 [8192], P(('batch', 'seq')), parts along dimension 0, may hold values from 0 to 4095, each once
- d_out: bfloat16 [2048, 1280], P(('batch', 'seq'), 'kvh'), parts along dimension 0, may hold values from -6 to 6
Outputs:
- attended: bfloat16 [2048, 1280], P(('batch', 'seq'), 'kvh'), parts along dimension 0
- grad_query: bfloat16 [2048, 1280], P(('batch', 'seq'), 'kvh'), parts along dimension 0
- grad_keys: bfloat16 [2048, 256], P(('batch', 'seq'), 'kvh'), parts along dimension 0
- grad_values: bfloat16 [2048, 256], P(('batch', 'seq'), 'kvh'), parts along dimension 0
There are 2 independent parts, one for each index of `batch`. A program takes and returns all parts, laid end to end along the dimension named above; each array names one. Nothing has to cross between parts.
Inputs may be any that keep to these rules, and one draw needn't show every extreme that they name: `cache_pos`: each cache position appears once.
All inputs are finite; a program needn't handle non-finite values.
Results may differ from a plain program's by a relative error of at most 0.012.
The roundings to bfloat16 on the way count: a program that leaves them out, or rounds other values in their place, can miss the bound.
Values may be sent and summed in bfloat16 or wider, within the bound.
A program may use at most 64 MiB of HBM per device.

v0:
```python
import jax
import jax.numpy as jnp
from jax import lax
from jax.sharding import PartitionSpec as P

HD = 128
GROUP = 5
WINDOW = 512


def shifted(block, axis, distance):
    devices = range(lax.axis_size(axis))
    route = [(i - distance, i) for i in devices if i - distance in devices]
    return lax.ppermute(block, axis, route)


def cache_limit(anchor, rows_dev, start_pos):
    row_index = anchor * rows_dev + jnp.arange(rows_dev, dtype=jnp.int32)
    return start_pos + jnp.maximum(row_index - WINDOW + 1, 0)


def forward_piece(partial_value, queries, bound_pos, key_rows, values, positions, scaling, final):
    scores = (
        jnp.einsum("tgd,cd->gtc", queries, key_rows, preferred_element_type=jnp.float32) * scaling
    )
    visible = positions[None, :] < bound_pos[:, None]
    scores = jnp.where(visible[None], scores, -jnp.inf)
    if not final:
        row_max, row_sum = partial_value
        new_max = jnp.maximum(row_max, jnp.max(scores, axis=2))
        factor = jnp.exp(row_max - new_max)
        row_sum = row_sum * factor + jnp.sum(jnp.exp(scores - new_max[:, :, None]), axis=2)
        return (new_max, row_sum)
    summed, log_total = partial_value
    weights = jnp.exp(scores - log_total[:, :, None]).astype(jnp.bfloat16)
    summed = summed + jnp.einsum("gtc,cd->gtd", weights, values, preferred_element_type=jnp.float32)
    return (summed, log_total)


def backward_piece(
    grad_acc,
    queries,
    grads_out,
    log_total,
    delta_rows,
    bound_pos,
    key_rows,
    values,
    positions,
    scaling,
):
    scores = (
        jnp.einsum("tgd,cd->gtc", queries, key_rows, preferred_element_type=jnp.float32) * scaling
    )
    visible = positions[None, :] < bound_pos[:, None]
    scores = jnp.where(visible[None], scores, -jnp.inf)
    weights = jnp.exp(scores - log_total[:, :, None])
    grad_weights = jnp.einsum("tgd,cd->gtc", grads_out, values, preferred_element_type=jnp.float32)
    grad_scores = (weights * (grad_weights - delta_rows[:, :, None])).astype(jnp.bfloat16)
    return grad_acc + jnp.einsum(
        "gtc,cd->tgd", grad_scores, key_rows, preferred_element_type=jnp.float32
    )


def local(query, self_keys, self_values, cache_keys, cache_values, cache_pos, d_out):
    rows_dev = query.shape[0]
    cache_dev = cache_keys.shape[0]
    cycle_size = lax.axis_size("seq")
    my_index = lax.axis_index("seq")
    start_pos = cache_dev * cycle_size - rows_dev * cycle_size
    scaling = HD ** (-0.5)
    queries = query.reshape(rows_dev, GROUP, HD)
    grads_out = d_out.reshape(rows_dev, GROUP, HD)
    rim_count = (WINDOW + rows_dev - 2) // rows_dev
    pair = (self_keys, self_values)
    moving = pair
    collected = []
    for distance in range(rim_count):
        moving = shifted((moving[0], moving[1]), "seq", 1)
        collected.append(moving)
    earlier = collected[::-1]
    window_keys = jnp.concatenate([member[0] for member in earlier] + [self_keys], axis=0)
    window_values = jnp.concatenate([member[1] for member in earlier] + [self_values], axis=0)
    window_rows = window_keys.shape[0]
    key_index = (my_index - rim_count) * rows_dev + jnp.arange(window_rows, dtype=jnp.int32)
    query_index = my_index * rows_dev + jnp.arange(rows_dev, dtype=jnp.int32)
    visible = (
        (key_index[None, :] <= query_index[:, None])
        & (key_index[None, :] >= query_index[:, None] - WINDOW + 1)
        & (key_index[None, :] >= 0)
    )
    scores = (
        jnp.einsum("tgd,cd->gtc", queries, window_keys, preferred_element_type=jnp.float32)
        * scaling
    )
    scores = jnp.where(visible[None], scores, -jnp.inf)
    row_max = jnp.max(scores, axis=2)
    row_sum = jnp.sum(jnp.exp(scores - row_max[:, :, None]), axis=2)
    own_limit = cache_limit(my_index, rows_dev, start_pos)
    all_positions = lax.all_gather(cache_pos, "seq", axis=0, tiled=True)

    def run_tour(partial_value, final):
        carried = partial_value
        key_part = lax.all_gather(cache_keys, "seq", axis=0, tiled=True)
        value_part = lax.all_gather(cache_values, "seq", axis=0, tiled=True)
        shard_count = key_part.shape[0] // cache_dev

        def one_shard(running, shard_data):
            return (
                forward_piece(
                    running,
                    queries,
                    own_limit,
                    shard_data[0],
                    shard_data[1],
                    shard_data[2],
                    scaling,
                    final,
                ),
                None,
            )

        carried, unused = lax.scan(
            one_shard,
            carried,
            (
                key_part.reshape(shard_count, cache_dev, HD),
                value_part.reshape(shard_count, cache_dev, HD),
                all_positions.reshape(shard_count, cache_dev),
            ),
        )
        return carried

    row_max, row_sum = run_tour((row_max, row_sum), False)
    log_total = row_max + jnp.log(row_sum)
    back_weights = jnp.exp(scores - log_total[:, :, None])
    back_rounded = back_weights.astype(jnp.bfloat16)
    summed = jnp.einsum(
        "gtc,cd->gtd", back_rounded, window_values, preferred_element_type=jnp.float32
    )
    summed, unused_total = run_tour((summed, log_total), True)
    attended = jnp.transpose(summed, (1, 0, 2)).astype(jnp.bfloat16)
    delta_rows = jnp.sum(grads_out.astype(jnp.float32) * attended.astype(jnp.float32), axis=2).T
    grad_weights = jnp.einsum(
        "tgd,cd->gtc", grads_out, window_values, preferred_element_type=jnp.float32
    )
    grad_scores = (back_weights * (grad_weights - delta_rows[:, :, None])).astype(jnp.bfloat16)
    grad_acc = jnp.einsum(
        "gtc,cd->tgd", grad_scores, window_keys, preferred_element_type=jnp.float32
    )
    key_grads = jnp.einsum("gtc,tgd->cd", grad_scores, queries, preferred_element_type=jnp.float32)
    value_grads = jnp.einsum(
        "gtc,tgd->cd", back_rounded, grads_out, preferred_element_type=jnp.float32
    )
    carried = grad_acc
    key_part = lax.all_gather(cache_keys, "seq", axis=0, tiled=True)
    value_part = lax.all_gather(cache_values, "seq", axis=0, tiled=True)
    shard_count = key_part.shape[0] // cache_dev

    def one_shard(running, shard_data):
        return (
            backward_piece(
                running,
                queries,
                grads_out,
                log_total,
                delta_rows,
                own_limit,
                shard_data[0],
                shard_data[1],
                shard_data[2],
                scaling,
            ),
            None,
        )

    carried, unused = lax.scan(
        one_shard,
        carried,
        (
            key_part.reshape(shard_count, cache_dev, HD),
            value_part.reshape(shard_count, cache_dev, HD),
            all_positions.reshape(shard_count, cache_dev),
        ),
    )
    grad_acc = carried
    key_blocks = key_grads.reshape(rim_count + 1, rows_dev, HD)
    value_blocks = value_grads.reshape(rim_count + 1, rows_dev, HD)
    carried = (key_blocks[0], value_blocks[0])
    for position in range(1, rim_count + 1):
        moved = (
            shifted(carried[0].astype(jnp.bfloat16), "seq", -1).astype(jnp.float32),
            shifted(carried[1].astype(jnp.bfloat16), "seq", -1).astype(jnp.float32),
        )
        carried = (moved[0] + key_blocks[position], moved[1] + value_blocks[position])
    total_keys, total_values = carried
    grad_query = (grad_acc * scaling).astype(jnp.bfloat16).reshape(rows_dev, GROUP * HD)
    grad_keys = (total_keys * scaling).astype(jnp.bfloat16)
    grad_values = total_values.astype(jnp.bfloat16)
    return (attended.reshape(rows_dev, GROUP * HD), grad_query, grad_keys, grad_values)


def solution(mesh):
    in_specs = (
        P(("batch", "seq"), "kvh"),
        P(("batch", "seq"), "kvh"),
        P(("batch", "seq"), "kvh"),
        P(("batch", "seq"), "kvh"),
        P(("batch", "seq"), "kvh"),
        P(("batch", "seq")),
        P(("batch", "seq"), "kvh"),
    )
    out_specs = (
        P(("batch", "seq"), "kvh"),
        P(("batch", "seq"), "kvh"),
        P(("batch", "seq"), "kvh"),
        P(("batch", "seq"), "kvh"),
    )
    return jax.shard_map(local, mesh=mesh, in_specs=in_specs, out_specs=out_specs, check_vma=False)
```

profile of v0, /device:TPU:19, one launch (start us, length us, event | category | flops | bytes accessed | tf_op | source)
XLA Modules:
  0.0 134.8 jit_solution(12396199009826512180)
XLA Ops:
  8.0 3.8 %collective-permute-start = (bf16[128,128]{1,0:T(8,128)(2,1)}, bf16[128,128]{1,0:T(8,128)(2,1)S(1)}, u32[]{:S(2)}, u32[]{:S(2)}) collective-permute-start(bf16[128,128]{1,0:T(8,128)(2,1)} %param.14), channel_id=1, source_target_pairs={{0,4},{4,8},{8,12},{12,16},{16,20},{20,24},{24,28},{1,5},{5,9},{9,... | collective-permute-start | bytes 98312 | tf_op jit(solution)/shard_map/ppermute | solution.py:14
  11.7 1.9 %collective-permute-start.4 = (bf16[128,128]{1,0:T(8,128)(2,1)}, bf16[128,128]{1,0:T(8,128)(2,1)S(1)}, u32[]{:S(2)}, u32[]{:S(2)}) collective-permute-start(bf16[128,128]{1,0:T(8,128)(2,1)} %param.15), channel_id=1, source_target_pairs={{0,4},{4,8},{8,12},{12,16},{16,20},{20,24},{24,28},{1,5},{5,9},{9,... | collective-permute-start | bytes 98312 | tf_op jit(solution)/shard_map/ppermute | solution.py:14
  13.7 3.4 %collective-permute-start.1 = (bf16[128,128]{1,0:T(8,128)(2,1)S(1)}, bf16[128,128]{1,0:T(8,128)(2,1)S(1)}, u32[]{:S(2)}, u32[]{:S(2)}) collective-permute-start(bf16[128,128]{1,0:T(8,128)(2,1)S(1)} %collective-permute-done), channel_id=1, source_target_pairs={{0,4},{4,8},{8,12},{12,16},{16,20},{20,24},{24,28},{1,5},{5,9},{9,... | collective-permute-start | bytes 98312 | tf_op jit(solution)/shard_map/ppermute | solution.py:14
  17.2 1.9 %collective-permute-start.5 = (bf16[128,128]{1,0:T(8,128)(2,1)S(1)}, bf16[128,128]{1,0:T(8,128)(2,1)S(1)}, u32[]{:S(2)}, u32[]{:S(2)}) collective-permute-start(bf16[128,128]{1,0:T(8,128)(2,1)S(1)} %collective-permute-done.4), channel_id=1, source_target_pairs={{0,4},{4,8},{8,12},{12,16},{16,20},{20,24},{24,28},{1,5},{5,9},{9,... | collective-permute-start | bytes 98312 | tf_op jit(solution)/shard_map/ppermute | solution.py:14
  19.1 3.2 %collective-permute-start.2 = (bf16[128,128]{1,0:T(8,128)(2,1)S(1)}, bf16[128,128]{1,0:T(8,128)(2,1)S(1)}, u32[]{:S(2)}, u32[]{:S(2)}) collective-permute-start(bf16[128,128]{1,0:T(8,128)(2,1)S(1)} %collective-permute-done.1), channel_id=1, source_target_pairs={{0,4},{4,8},{8,12},{12,16},{16,20},{20,24},{24,28},{1,5},{5,9},{9,... | collective-permute-start | bytes 98312 | tf_op jit(solution)/shard_map/ppermute | solution.py:14
  22.4 2.8 %collective-permute-start.6 = (bf16[128,128]{1,0:T(8,128)(2,1)S(1)}, bf16[128,128]{1,0:T(8,128)(2,1)S(1)}, u32[]{:S(2)}, u32[]{:S(2)}) collective-permute-start(bf16[128,128]{1,0:T(8,128)(2,1)S(1)} %collective-permute-done.5), channel_id=1, source_target_pairs={{0,4},{4,8},{8,12},{12,16},{16,20},{20,24},{24,28},{1,5},{5,9},{9,... | collective-permute-start | bytes 98312 | tf_op jit(solution)/shard_map/ppermute | solution.py:14
  25.3 2.9 %collective-permute-start.3 = (bf16[128,128]{1,0:T(8,128)(2,1)S(1)}, bf16[128,128]{1,0:T(8,128)(2,1)S(1)}, u32[]{:S(2)}, u32[]{:S(2)}) collective-permute-start(bf16[128,128]{1,0:T(8,128)(2,1)S(1)} %collective-permute-done.2), channel_id=1, source_target_pairs={{0,4},{4,8},{8,12},{12,16},{16,20},{20,24},{24,28},{1,5},{5,9},{9,... | collective-permute-start | bytes 98312 | tf_op jit(solution)/shard_map/ppermute | solution.py:14
  29.6 10.7 %all-gather = s32[8,1,512]{2,1,0:T(1,128)S(1)} all-gather(s32[1,1,512]{2,1,0:T(1,128)} %bitcast.177), channel_id=1, replica_groups=mesh['seq'=8,'kvh'=2,'batch'=2] {'seq'}, dimensions={0}, use_global_device_ids=true | all-gather | bytes 18432 | tf_op jit(solution)/shard_map/all_gather | solution.py:100
  41.7 2.8 %collective-permute-start.7 = (bf16[128,128]{1,0:T(8,128)(2,1)S(1)}, bf16[128,128]{1,0:T(8,128)(2,1)S(1)}, u32[]{:S(2)}, u32[]{:S(2)}) collective-permute-start(bf16[128,128]{1,0:T(8,128)(2,1)S(1)} %collective-permute-done.6), channel_id=1, source_target_pairs={{0,4},{4,8},{8,12},{12,16},{16,20},{20,24},{24,28},{1,5},{5,9},{9,... | collective-permute-start | bytes 98312 | tf_op jit(solution)/shard_map/ppermute | solution.py:14
  44.5 1.9 %collective-permute-done.7 = bf16[128,128]{1,0:T(8,128)(2,1)S(1)} collective-permute-done((bf16[128,128]{1,0:T(8,128)(2,1)S(1)}, bf16[128,128]{1,0:T(8,128)(2,1)S(1)}, u32[]{:S(2)}, u32[]{:S(2)}) %collective-permute-start.7) | collective-permute-done | bytes 32800 | tf_op jit(solution)/shard_map/ppermute | solution.py:14
  47.1 13.4 %while.35 = (s32[]{:T(128)}, f32[5,128]{1,0:T(8,128)S(1)}, f32[5,128]{1,0:T(8,128)S(1)}, s32[8,512]{1,0:T(8,128)S(1)}, bf16[8,512,128]{2,1,0:T(8,128)(2,1)}, /*i...) while((s32[]{:T(128)}, f32[5,128]{1,0:T(8,128)S(1)}, f32[5,128]{1,0:T(8,128)S(1)}, ...), condition=%wide.region_5.6_spmd.clone, body=%wide.region_2.5_spmd.clone.sunk | while | flops 85591808 | bytes 3088477 | solution.py:123
  61.4 14.7 %while.36 = (s32[]{:T(128)}, f32[5,128,128]{2,1,0:T(8,128)S(1)}, s32[8,512]{1,0:T(8,128)S(1)}, bf16[8,512,128]{2,1,0:T(8,128)(2,1)}, bf16[128,5,128]{2,0,1:T(8,1...) while((s32[]{:T(128)}, f32[5,128,128]{2,1,0:T(8,128)S(1)}, ...), condition=%wide.region_7.8_spmd.clone, body=%wide.region_6.7_spmd.clone.sunk | while | flops 169230848 | bytes 1223269 | solution.py:123
  65.3 1.7 %fusion.103 = f32[5,128,128]{2,1,0:T(8,128)S(1)} fusion(f32[5,128,128]{2,1,0:T(8,128)S(1)} %get-tuple-element.519, bf16[128,5,128]{2,0,1:T(8,128)(2,1)S(1)} %get-tuple-element.531, f32[5,128]{1,0:T(8,128)S(1)} %get-tuple-element.532, pred[128,512]{0,1:T(8,128)(4,1)S(1)} %broadcast_compare_fusion.8, bf16[8,512,128]{2,1,0:T(8,128)(2,1)} %get-tuple-element.533, ...), kind=kOutput, calls=%fused_computation.21.clone.1 | convolution fusion | flops 169164800 | bytes 1150464 | tf_op jit(solution)/shard_map/while/body/eval_jaxpr/gtc,cd->gtd/dot_general | solution.py:36
  69.0 1.7 %fusion.103 = f32[5,128,128]{2,1,0:T(8,128)S(1)} fusion(f32[5,128,128]{2,1,0:T(8,128)S(1)} %get-tuple-element.519, bf16[128,5,128]{2,0,1:T(8,128)(2,1)S(1)} %get-tuple-element.531, f32[5,128]{1,0:T(8,128)S(1)} %get-tuple-element.532, pred[128,512]{0,1:T(8,128)(4,1)S(1)} %broadcast_compare_fusion.8, bf16[8,512,128]{2,1,0:T(8,128)(2,1)} %get-tuple-element.533, ...), kind=kOutput, calls=%fused_computation.21.clone.1 | convolution fusion | flops 169164800 | bytes 1150464 | tf_op jit(solution)/shard_map/while/body/eval_jaxpr/gtc,cd->gtd/dot_general | solution.py:36
  77.6 3.2 %collective-permute-start.12 = (bf16[128,128]{1,0:T(8,128)(2,1)S(1)}, bf16[128,128]{1,0:T(8,128)(2,1)S(1)}, u32[]{:S(2)}, u32[]{:S(2)}) collective-permute-start(bf16[128,128]{1,0:T(8,128)(2,1)S(1)} %slice.90), channel_id=1, source_target_pairs={{4,0},{8,4},{12,8},{16,12},{20,16},{24,20},{28,24},{5,1},{9,5},{13... | collective-permute-start | bytes 98312 | tf_op jit(solution)/shard_map/ppermute | solution.py:14
  80.9 1.9 %collective-permute-start.8 = (bf16[128,128]{1,0:T(8,128)(2,1)S(1)}, bf16[128,128]{1,0:T(8,128)(2,1)S(1)}, u32[]{:S(2)}, u32[]{:S(2)}) collective-permute-start(bf16[128,128]{1,0:T(8,128)(2,1)S(1)} %slice.91), channel_id=1, source_target_pairs={{4,0},{8,4},{12,8},{16,12},{20,16},{24,20},{28,24},{5,1},{9,5},{13... | collective-permute-start | bytes 98312 | tf_op jit(solution)/shard_map/ppermute | solution.py:14
  82.8 24.3 %while.37 = (s32[]{:T(128)}, f32[128,5,128]{0,2,1:T(8,128)S(1)}, bf16[8,512,128]{2,1,0:T(8,128)(2,1)}, s32[8,512]{1,0:T(8,128)S(1)}, bf16[128,5,128]{2,0,1:T(8,1...) while((s32[]{:T(128)}, f32[128,5,128]{0,2,1:T(8,128)S(1)}, ...), condition=%wide.region_10.11_spmd.clone, body=%wide.region_9.10_spmd.clone.sunk | while | flops 253772288 | bytes 4142709 | solution.py:177
  108.8 2.8 %collective-permute-start.13 = (bf16[128,128]{1,0:T(8,128)(2,1)S(1)}, bf16[128,128]{1,0:T(8,128)(2,1)S(1)}, u32[]{:S(2)}, u32[]{:S(2)}) collective-permute-start(bf16[128,128]{1,0:T(8,128)(2,1)S(1)} %fusion.67), channel_id=1, source_target_pairs={{4,0},{8,4},{12,8},{16,12},{20,16},{24,20},{28,24},{5,1},{9,5},{13... | collective-permute-start | bytes 98312 | tf_op jit(solution)/shard_map/ppermute | solution.py:14
  111.6 1.9 %collective-permute-start.9 = (bf16[128,128]{1,0:T(8,128)(2,1)S(1)}, bf16[128,128]{1,0:T(8,128)(2,1)S(1)}, u32[]{:S(2)}, u32[]{:S(2)}) collective-permute-start(bf16[128,128]{1,0:T(8,128)(2,1)S(1)} %fusion.72), channel_id=1, source_target_pairs={{4,0},{8,4},{12,8},{16,12},{20,16},{24,20},{28,24},{5,1},{9,5},{13... | collective-permute-start | bytes 98312 | tf_op jit(solution)/shard_map/ppermute | solution.py:14
  114.0 1.9 %collective-permute-start.14 = (bf16[128,128]{1,0:T(8,128)(2,1)S(1)}, bf16[128,128]{1,0:T(8,128)(2,1)S(1)}, u32[]{:S(2)}, u32[]{:S(2)}) collective-permute-start(bf16[128,128]{1,0:T(8,128)(2,1)S(1)} %fusion.66), channel_id=1, source_target_pairs={{4,0},{8,4},{12,8},{16,12},{20,16},{24,20},{28,24},{5,1},{9,5},{13... | collective-permute-start | bytes 98312 | tf_op jit(solution)/shard_map/ppermute | solution.py:14
  116.9 1.9 %collective-permute-start.10 = (bf16[128,128]{1,0:T(8,128)(2,1)S(1)}, bf16[128,128]{1,0:T(8,128)(2,1)S(1)}, u32[]{:S(2)}, u32[]{:S(2)}) collective-permute-start(bf16[128,128]{1,0:T(8,128)(2,1)S(1)} %fusion.71), channel_id=1, source_target_pairs={{4,0},{8,4},{12,8},{16,12},{20,16},{24,20},{28,24},{5,1},{9,5},{13... | collective-permute-start | bytes 98312 | tf_op jit(solution)/shard_map/ppermute | solution.py:14
  119.3 1.9 %collective-permute-start.15 = (bf16[128,128]{1,0:T(8,128)(2,1)S(1)}, bf16[128,128]{1,0:T(8,128)(2,1)S(1)}, u32[]{:S(2)}, u32[]{:S(2)}) collective-permute-start(bf16[128,128]{1,0:T(8,128)(2,1)S(1)} %fusion.65), channel_id=1, source_target_pairs={{4,0},{8,4},{12,8},{16,12},{20,16},{24,20},{28,24},{5,1},{9,5},{13... | collective-permute-start | bytes 98312 | tf_op jit(solution)/shard_map/ppermute | solution.py:14
  122.1 1.9 %collective-permute-start.11 = (bf16[128,128]{1,0:T(8,128)(2,1)S(1)}, bf16[128,128]{1,0:T(8,128)(2,1)S(1)}, u32[]{:S(2)}, u32[]{:S(2)}) collective-permute-start(bf16[128,128]{1,0:T(8,128)(2,1)S(1)} %fusion.70), channel_id=1, source_target_pairs={{4,0},{8,4},{12,8},{16,12},{20,16},{24,20},{28,24},{5,1},{9,5},{13... | collective-permute-start | bytes 98312 | tf_op jit(solution)/shard_map/ppermute | solution.py:14
  125.1 2.2 %collective-permute-done.11 = bf16[128,128]{1,0:T(8,128)(2,1)S(1)} collective-permute-done((bf16[128,128]{1,0:T(8,128)(2,1)S(1)}, bf16[128,128]{1,0:T(8,128)(2,1)S(1)}, u32[]{:S(2)}, u32[]{:S(2)}) %collective-permute-start.11) | collective-permute-done | bytes 32800 | tf_op jit(solution)/shard_map/ppermute | solution.py:14
  (200 shorter events, 60.5 us)
Async XLA Ops:
  7.2 37.3 %copy-start = (bf16[128,128]{1,0:T(8,128)(2,1)S(1)}, bf16[128,128]{1,0:T(8,128)(2,1)}, u32[]{:S(2)}) copy-start(bf16[128,128]{1,0:T(8,128)(2,1)} %param.14) | copy-start | bytes 98308
  7.2 39.3 %copy-start.1 = (bf16[128,128]{1,0:T(8,128)(2,1)S(1)}, bf16[128,128]{1,0:T(8,128)(2,1)}, u32[]{:S(2)}) copy-start(bf16[128,128]{1,0:T(8,128)(2,1)} %param.15) | copy-start | bytes 98308
  7.2 39.9 %all-gather.4.cloned.1.call-start = ((), (), s32[]{:S(2)}) async-start(), calls=%async_computation | async-start | bytes 1179648 | tf_op jit(solution)/shard_map/all_gather | solution.py:104
  7.9 53.5 %all-gather.6.cloned.1.call-start = ((), (), s32[]{:S(2)}) async-start(), calls=%async_computation.1 | async-start | bytes 1179648 | tf_op jit(solution)/shard_map/all_gather | solution.py:105
  8.0 5.7 %collective-permute-start = (bf16[128,128]{1,0:T(8,128)(2,1)}, bf16[128,128]{1,0:T(8,128)(2,1)S(1)}, u32[]{:S(2)}, u32[]{:S(2)}) collective-permute-start(bf16[128,128]{1,0:T(8,128)(2,1)} %param.14), channel_id=1, source_target_pairs={{0,4},{4,8},{8,12},{12,16},{16,20},{20,24},{24,28},{1,5},{5,9},{9,... | collective-permute-start | bytes 98312 | tf_op jit(solution)/shard_map/ppermute | solution.py:14
  11.7 5.5 %collective-permute-start.4 = (bf16[128,128]{1,0:T(8,128)(2,1)}, bf16[128,128]{1,0:T(8,128)(2,1)S(1)}, u32[]{:S(2)}, u32[]{:S(2)}) collective-permute-start(bf16[128,128]{1,0:T(8,128)(2,1)} %param.15), channel_id=1, source_target_pairs={{0,4},{4,8},{8,12},{12,16},{16,20},{20,24},{24,28},{1,5},{5,9},{9,... | collective-permute-start | bytes 98312 | tf_op jit(solution)/shard_map/ppermute | solution.py:14
  13.7 5.4 %collective-permute-start.1 = (bf16[128,128]{1,0:T(8,128)(2,1)S(1)}, bf16[128,128]{1,0:T(8,128)(2,1)S(1)}, u32[]{:S(2)}, u32[]{:S(2)}) collective-permute-start(bf16[128,128]{1,0:T(8,128)(2,1)S(1)} %collective-permute-done), channel_id=1, source_target_pairs={{0,4},{4,8},{8,12},{12,16},{16,20},{20,24},{24,28},{1,5},{5,9},{9,... | collective-permute-start | bytes 98312 | tf_op jit(solution)/shard_map/ppermute | solution.py:14
  17.2 5.2 %collective-permute-start.5 = (bf16[128,128]{1,0:T(8,128)(2,1)S(1)}, bf16[128,128]{1,0:T(8,128)(2,1)S(1)}, u32[]{:S(2)}, u32[]{:S(2)}) collective-permute-start(bf16[128,128]{1,0:T(8,128)(2,1)S(1)} %collective-permute-done.4), channel_id=1, source_target_pairs={{0,4},{4,8},{8,12},{12,16},{16,20},{20,24},{24,28},{1,5},{5,9},{9,... | collective-permute-start | bytes 98312 | tf_op jit(solution)/shard_map/ppermute | solution.py:14
  19.1 6.1 %collective-permute-start.2 = (bf16[128,128]{1,0:T(8,128)(2,1)S(1)}, bf16[128,128]{1,0:T(8,128)(2,1)S(1)}, u32[]{:S(2)}, u32[]{:S(2)}) collective-permute-start(bf16[128,128]{1,0:T(8,128)(2,1)S(1)} %collective-permute-done.1), channel_id=1, source_target_pairs={{0,4},{4,8},{8,12},{12,16},{16,20},{20,24},{24,28},{1,5},{5,9},{9,... | collective-permute-start | bytes 98312 | tf_op jit(solution)/shard_map/ppermute | solution.py:14
  22.4 19.2 %collective-permute-start.6 = (bf16[128,128]{1,0:T(8,128)(2,1)S(1)}, bf16[128,128]{1,0:T(8,128)(2,1)S(1)}, u32[]{:S(2)}, u32[]{:S(2)}) collective-permute-start(bf16[128,128]{1,0:T(8,128)(2,1)S(1)} %collective-permute-done.5), channel_id=1, source_target_pairs={{0,4},{4,8},{8,12},{12,16},{16,20},{20,24},{24,28},{1,5},{5,9},{9,... | collective-permute-start | bytes 98312 | tf_op jit(solution)/shard_map/ppermute | solution.py:14
  25.3 19.2 %collective-permute-start.3 = (bf16[128,128]{1,0:T(8,128)(2,1)S(1)}, bf16[128,128]{1,0:T(8,128)(2,1)S(1)}, u32[]{:S(2)}, u32[]{:S(2)}) collective-permute-start(bf16[128,128]{1,0:T(8,128)(2,1)S(1)} %collective-permute-done.2), channel_id=1, source_target_pairs={{0,4},{4,8},{8,12},{12,16},{16,20},{20,24},{24,28},{1,5},{5,9},{9,... | collective-permute-start | bytes 98312 | tf_op jit(solution)/shard_map/ppermute | solution.py:14
  41.7 4.7 %collective-permute-start.7 = (bf16[128,128]{1,0:T(8,128)(2,1)S(1)}, bf16[128,128]{1,0:T(8,128)(2,1)S(1)}, u32[]{:S(2)}, u32[]{:S(2)}) collective-permute-start(bf16[128,128]{1,0:T(8,128)(2,1)S(1)} %collective-permute-done.6), channel_id=1, source_target_pairs={{0,4},{4,8},{8,12},{12,16},{16,20},{20,24},{24,28},{1,5},{5,9},{9,... | collective-permute-start | bytes 98312 | tf_op jit(solution)/shard_map/ppermute | solution.py:14
  77.6 31.1 %collective-permute-start.12 = (bf16[128,128]{1,0:T(8,128)(2,1)S(1)}, bf16[128,128]{1,0:T(8,128)(2,1)S(1)}, u32[]{:S(2)}, u32[]{:S(2)}) collective-permute-start(bf16[128,128]{1,0:T(8,128)(2,1)S(1)} %slice.90), channel_id=1, source_target_pairs={{4,0},{8,4},{12,8},{16,12},{20,16},{24,20},{28,24},{5,1},{9,5},{13... | collective-permute-start | bytes 98312 | tf_op jit(solution)/shard_map/ppermute | solution.py:14
  80.9 30.8 %collective-permute-start.8 = (bf16[128,128]{1,0:T(8,128)(2,1)S(1)}, bf16[128,128]{1,0:T(8,128)(2,1)S(1)}, u32[]{:S(2)}, u32[]{:S(2)}) collective-permute-start(bf16[128,128]{1,0:T(8,128)(2,1)S(1)} %slice.91), channel_id=1, source_target_pairs={{4,0},{8,4},{12,8},{16,12},{20,16},{24,20},{28,24},{5,1},{9,5},{13... | collective-permute-start | bytes 98312 | tf_op jit(solution)/shard_map/ppermute | solution.py:14
  108.8 5.2 %collective-permute-start.13 = (bf16[128,128]{1,0:T(8,128)(2,1)S(1)}, bf16[128,128]{1,0:T(8,128)(2,1)S(1)}, u32[]{:S(2)}, u32[]{:S(2)}) collective-permute-start(bf16[128,128]{1,0:T(8,128)(2,1)S(1)} %fusion.67), channel_id=1, source_target_pairs={{4,0},{8,4},{12,8},{16,12},{20,16},{24,20},{28,24},{5,1},{9,5},{13... | collective-permute-start | bytes 98312 | tf_op jit(solution)/shard_map/ppermute | solution.py:14
  111.6 5.2 %collective-permute-start.9 = (bf16[128,128]{1,0:T(8,128)(2,1)S(1)}, bf16[128,128]{1,0:T(8,128)(2,1)S(1)}, u32[]{:S(2)}, u32[]{:S(2)}) collective-permute-start(bf16[128,128]{1,0:T(8,128)(2,1)S(1)} %fusion.72), channel_id=1, source_target_pairs={{4,0},{8,4},{12,8},{16,12},{20,16},{24,20},{28,24},{5,1},{9,5},{13... | collective-permute-start | bytes 98312 | tf_op jit(solution)/shard_map/ppermute | solution.py:14
  114.0 5.2 %collective-permute-start.14 = (bf16[128,128]{1,0:T(8,128)(2,1)S(1)}, bf16[128,128]{1,0:T(8,128)(2,1)S(1)}, u32[]{:S(2)}, u32[]{:S(2)}) collective-permute-start(bf16[128,128]{1,0:T(8,128)(2,1)S(1)} %fusion.66), channel_id=1, source_target_pairs={{4,0},{8,4},{12,8},{16,12},{20,16},{24,20},{28,24},{5,1},{9,5},{13... | collective-permute-start | bytes 98312 | tf_op jit(solution)/shard_map/ppermute | solution.py:14
  116.9 5.2 %collective-permute-start.10 = (bf16[128,128]{1,0:T(8,128)(2,1)S(1)}, bf16[128,128]{1,0:T(8,128)(2,1)S(1)}, u32[]{:S(2)}, u32[]{:S(2)}) collective-permute-start(bf16[128,128]{1,0:T(8,128)(2,1)S(1)} %fusion.71), channel_id=1, source_target_pairs={{4,0},{8,4},{12,8},{16,12},{20,16},{24,20},{28,24},{5,1},{9,5},{13... | collective-permute-start | bytes 98312 | tf_op jit(solution)/shard_map/ppermute | solution.py:14
  119.3 5.2 %collective-permute-start.15 = (bf16[128,128]{1,0:T(8,128)(2,1)S(1)}, bf16[128,128]{1,0:T(8,128)(2,1)S(1)}, u32[]{:S(2)}, u32[]{:S(2)}) collective-permute-start(bf16[128,128]{1,0:T(8,128)(2,1)S(1)} %fusion.65), channel_id=1, source_target_pairs={{4,0},{8,4},{12,8},{16,12},{20,16},{24,20},{28,24},{5,1},{9,5},{13... | collective-permute-start | bytes 98312 | tf_op jit(solution)/shard_map/ppermute | solution.py:14
  122.1 5.2 %collective-permute-start.11 = (bf16[128,128]{1,0:T(8,128)(2,1)S(1)}, bf16[128,128]{1,0:T(8,128)(2,1)S(1)}, u32[]{:S(2)}, u32[]{:S(2)}) collective-permute-start(bf16[128,128]{1,0:T(8,128)(2,1)S(1)} %fusion.70), channel_id=1, source_target_pairs={{4,0},{8,4},{12,8},{16,12},{20,16},{24,20},{28,24},{5,1},{9,5},{13... | collective-permute-start | bytes 98312 | tf_op jit(solution)/shard_map/ppermute | solution.py:14
Sparse Core Ops, SparseCore 0:
  9.6 23.6 all-gather.3
  34.9 21.6 all-gather.5
where the time goes:
time: 136 us; the launch traced here: 135 us
  matrix products  48.3 us (36%)
  starting transfers between devices  40.4 us (30%)
  between operations  14.5 us (11%)
  blocking collectives  10.7 us (8%)
  waiting for transfers between devices  8.02 us (6%)
  other arithmetic  6.93 us (5%)
  local copies, waits for them, and re-layouts  4.61 us (3%)
    ppermute x16, starting transfers between devices, shifted(): return lax.ppermute(block, axis, route)  40.3 us
    dot_general x8, matrix products, forward_piece(): jnp.einsum('gtc,cd->gtd', weights, values, preferred_element_type=jnp.flo...  13.2 us
    dot_general x8, matrix products, backward_piece(): jnp.einsum('gtc,cd->tgd', grad_scores, key_rows, preferred_element_type=j...  12 us
    all_gather x1, blocking collectives, local(): all_positions = lax.all_gather(cache_pos, 'seq', axis=0, tiled=True)  10.7 us
    dot_general x8, matrix products, backward_piece(): jnp.einsum('tgd,cd->gtc', queries, key_rows, preferred_element_type=jnp.f...  10.7 us
    dot_general x8, matrix products, forward_piece(): jnp.einsum('tgd,cd->gtc', queries, key_rows, preferred_element_type=jnp.f...  10 us
    ppermute x16, waiting for transfers between devices, shifted(): return lax.ppermute(block, axis, route)  7.28 us
    unnamed x19, local copies, waits for them, and re-layouts  4.21 us
  transfers between devices with their start and end apart: 18, of which 7 were waited for; matrix products, arithmetic and copies ran while one was open for 32% of the time, Pallas kernels for 0%

commit v1 on v0

v1 whole, which is shorter than its diff:
```python
import functools
import math

import jax
import jax.numpy as jnp
from jax import lax
from jax.experimental import pallas as pl
from jax.experimental.pallas import tpu as pltpu
from jax.sharding import PartitionSpec as P

HD = 128
GROUP = 5
WINDOW = 512
NEG = -1e30
F32 = jnp.float32
BF16 = jnp.bfloat16
MESH = pl.DeviceIdType.MESH

LAST = (((1,), (1,)), ((), ()))
FIRST = (((0,), (0,)), ((), ()))


def dot_nt(a, b):
    return lax.dot_general(a, b, LAST, preferred_element_type=F32)


def dot_tn(a, b):
    return lax.dot_general(a, b, FIRST, preferred_element_type=F32)


def dot_nn(a, b):
    return jnp.dot(a, b, preferred_element_type=F32)


def lane_tiles(x, op):
    parts = [x[:, i : i + 128] for i in range(0, x.shape[1], 128)]
    return functools.reduce(op, parts)


def kernel(
    n, q_ref, sk_ref, sv_ref, ck_ref, cv_ref, cp_ref, do_ref,
    att_ref, dq_ref, dk_ref, dv_ref,
    qs, ds_out, kbuf, vbuf, pos, s_ref, dp_ref, sw_ref, m_ref, l_ref, acc,
    gk_send, gv_send, gk_recv, gv_recv,
    send_sem, recv_sem, pos_send, pos_recv, g_send, g_recv,
):
    rows = q_ref.shape[0]
    cached = ck_ref.shape[0]
    rim = (WINDOW + rows - 2) // rows
    rim_chips = (rim + 1) // 2
    chips = n // 2
    start_pos = (cached - rows) * n
    scale = HD ** -0.5
    scale2 = scale * math.log2(math.e)

    me = lax.axis_index("seq")
    z = me // 2
    core = me % 2
    sib = z * 2 + (1 - core)

    bufs = (kbuf, vbuf)
    kbuf[me, 0:cached] = ck_ref[...]
    kbuf[me, cached:] = sk_ref[...]
    vbuf[me, 0:cached] = cv_ref[...]
    vbuf[me, cached:] = sv_ref[...]
    pos[me] = cp_ref[...]

    barrier = pltpu.get_barrier_semaphore()
    for k in range(1, n):
        pl.semaphore_signal(
            barrier, inc=1, device_id={"seq": (me + k) % n}, device_id_type=MESH
        )
    pl.semaphore_wait(barrier, n - 1)

    def block_copy(a, way, o, size, target):
        part = bufs[a].at[o, pl.ds(0, size)]
        return pltpu.make_async_remote_copy(
            src_ref=part,
            dst_ref=part,
            send_sem=send_sem.at[a, way, o],
            recv_sem=recv_sem.at[a, o],
            device_id={"seq": target},
            device_id_type=MESH,
        )

    full = cached + rows

    def sized(near, run):
        @pl.when(near)
        def _():
            run(full)

        @pl.when(jnp.logical_not(near))
        def _():
            run(cached)

    def relay(a, t, act):
        left = me - 2 * t
        right = me + 2 * t

        def push(way, o, size, target):
            copy = block_copy(a, way, o, size, target)
            if act == "go":
                copy.start()
            else:
                copy.wait_send()

        @pl.when(z - t >= 0)
        def _():
            if act == "go":
                @pl.when(t > 0)
                def _():
                    sized(t <= rim_chips, lambda size: block_copy(a, 0, left, size, sib).wait_recv())

            @pl.when(z < chips - 1)
            def _():
                sized(t + 1 <= rim_chips, lambda size: push(0, left, size, me + 2))

            @pl.when(t == 0)
            def _():
                @pl.when(z > 0)
                def _():
                    push(1, left, cached, me - 2)

            sized(t <= rim_chips, lambda size: push(2, left, size, sib))

        @pl.when((t > 0) & (z + t < chips))
        def _():
            if act == "go":
                block_copy(a, 1, right, cached, sib).wait_recv()

            @pl.when(z > 0)
            def _():
                push(1, right, cached, me - 2)

            push(2, right, cached, sib)

    def consume(a, t, use):
        left = me - 2 * t
        right = me + 2 * t
        left_sib = left + sib - me
        right_sib = right + sib - me

        @pl.when(z - t >= 0)
        def _():
            use(left)

        @pl.when((t > 0) & (z + t < chips))
        def _():
            use(right)

        @pl.when(z - t >= 0)
        def _():
            sized(t <= rim_chips, lambda size: block_copy(a, 0, left_sib, size, sib).wait_recv())
            use(left_sib)

        @pl.when((t > 0) & (z + t < chips))
        def _():
            block_copy(a, 0, right_sib, cached, sib).wait_recv()
            use(right_sib)

    def pos_copy(o, target):
        return pltpu.make_async_remote_copy(
            src_ref=pos.at[o],
            dst_ref=pos.at[o],
            send_sem=pos_send.at[target],
            recv_sem=pos_recv.at[o],
            device_id={"seq": target},
            device_id_type=MESH,
        )

    relay(0, 0, "go")
    for k in range(1, n):
        pos_copy(me, (me + k) % n).start()

    def head(g):
        return slice(g * rows, (g + 1) * rows)

    for g in range(GROUP):
        qs[head(g)] = q_ref[:, g * HD : (g + 1) * HD]
        ds_out[head(g)] = do_ref[:, g * HD : (g + 1) * HD]
    m_ref[...] = jnp.full(m_ref.shape, NEG, F32)
    l_ref[...] = jnp.zeros(l_ref.shape, F32)
    acc[...] = jnp.zeros(acc.shape, F32)

    row_index = me * rows + lax.broadcasted_iota(jnp.int32, (rows, 1), 0)
    bound = start_pos + jnp.maximum(row_index - WINDOW + 1, 0)

    def score_shard(o):
        @pl.when(o != me)
        def _():
            pos_copy(o, sib).wait_recv()

        vis = pos[o] < bound
        for g in range(GROUP):
            s = dot_nt(qs[head(g)], kbuf[o, 0:cached])
            s = jnp.where(vis, s, NEG)
            s_ref[o, head(g)] = s
            m_ref[head(g)] = jnp.maximum(m_ref[head(g)], lane_tiles(s, jnp.maximum))

    @pl.loop(0, chips)
    def _(t):
        @pl.when(t > 0)
        def _():
            relay(0, t, "go")

        @pl.when(t == 1)
        def _():
            relay(1, 0, "go")

        consume(0, t, score_shard)

    first = jnp.maximum(me - rim, 0)
    delta_index = lax.broadcasted_iota(jnp.int32, (rows, rows), 0) - lax.broadcasted_iota(
        jnp.int32, (rows, rows), 1
    )

    @pl.loop(first, me + 1)
    def _(o):
        d = me - o
        gap = delta_index + d * rows
        vis = (gap >= 0) & (gap < WINDOW)
        for g in range(GROUP):
            s = dot_nt(qs[head(g)], kbuf[o, cached:])
            s = jnp.where(vis, s, NEG)
            sw_ref[d, head(g)] = s
            m_ref[head(g)] = jnp.maximum(m_ref[head(g)], s)

    for g in range(GROUP):
        top = jnp.max(m_ref[head(g)], axis=1, keepdims=True)
        m_ref[head(g)] = jnp.broadcast_to(top, (rows, 128))

    @pl.loop(0, n)
    def _(o):
        for g in range(GROUP):
            p = jnp.exp2((s_ref[o, head(g)] - m_ref[head(g), 0:1]) * scale2)
            s_ref[o, head(g)] = p
            l_ref[head(g)] += lane_tiles(p, jnp.add)

    @pl.loop(first, me + 1)
    def _(o):
        d = me - o
        for g in range(GROUP):
            p = jnp.exp2((sw_ref[d, head(g)] - m_ref[head(g)]) * scale2)
            sw_ref[d, head(g)] = p
            l_ref[head(g)] += p

    for g in range(GROUP):
        total = jnp.sum(l_ref[head(g)], axis=1, keepdims=True)
        l_ref[head(g)] = jnp.broadcast_to(1.0 / total, (rows, 128))

    def grad_copy(a, d, target):
        sent, got = ((gk_send, gk_recv), (gv_send, gv_recv))[a]
        return pltpu.make_async_remote_copy(
            src_ref=sent.at[d],
            dst_ref=got.at[d],
            send_sem=g_send.at[a, d],
            recv_sem=g_recv.at[a, d],
            device_id={"seq": target},
            device_id_type=MESH,
        )

    @pl.loop(first, me + 1)
    def _(o):
        d = me - o
        total = jnp.zeros((rows, HD), F32)
        for g in range(GROUP):
            w = sw_ref[d, head(g)] * l_ref[head(g)]
            sw_ref[d, head(g)] = w
            total = total + dot_tn(w.astype(BF16), ds_out[head(g)])
        gv_send[d] = total.astype(BF16)

        @pl.when(d == 0)
        def _():
            dv_ref[...] = total

        @pl.when(d > 0)
        def _():
            grad_copy(1, d, o).start()

    def value_shard(o):
        v = vbuf[o, 0:cached]
        for g in range(GROUP):
            w = s_ref[o, head(g)] * l_ref[head(g), 0:1]
            acc[head(g)] += dot_nn(w.astype(BF16), v)
            dp_ref[o, head(g)] = dot_nt(ds_out[head(g)], v)

    @pl.loop(0, chips)
    def _(t):
        @pl.when(t > 0)
        def _():
            relay(1, t, "go")

        consume(1, t, value_shard)

    @pl.loop(first, me + 1)
    def _(o):
        d = me - o
        v = vbuf[o, cached:]
        for g in range(GROUP):
            acc[head(g)] += dot_nn(sw_ref[d, head(g)].astype(BF16), v)

    for g in range(GROUP):
        out = acc[head(g)].astype(BF16)
        att_ref[:, g * HD : (g + 1) * HD] = out
        delta = jnp.sum(ds_out[head(g)].astype(F32) * out.astype(F32), axis=1, keepdims=True)
        m_ref[head(g)] = jnp.broadcast_to(delta, (rows, 128))
    acc[...] = jnp.zeros(acc.shape, F32)

    @pl.loop(first, me + 1)
    def _(o):
        d = me - o
        v = vbuf[o, cached:]
        key = kbuf[o, cached:]
        total = jnp.zeros((rows, HD), F32)
        for g in range(GROUP):
            dp = dot_nt(ds_out[head(g)], v)
            gs = (sw_ref[d, head(g)] * (dp - m_ref[head(g)])).astype(BF16)
            total = total + dot_tn(gs, qs[head(g)])
            acc[head(g)] += dot_nn(gs, key)
        gk_send[d] = total.astype(BF16)

        @pl.when(d == 0)
        def _():
            dk_ref[...] = total

        @pl.when(d > 0)
        def _():
            grad_copy(0, d, o).start()

    @pl.loop(0, n)
    def _(o):
        key = kbuf[o, 0:cached]
        for g in range(GROUP):
            w = s_ref[o, head(g)] * l_ref[head(g), 0:1]
            gs = (w * (dp_ref[o, head(g)] - m_ref[head(g), 0:1])).astype(BF16)
            acc[head(g)] += dot_nn(gs, key)

    for g in range(GROUP):
        dq_ref[:, g * HD : (g + 1) * HD] = (acc[head(g)] * scale).astype(BF16)

    @pl.loop(0, chips)
    def _(t):
        relay(0, t, "end")
        relay(1, t, "end")

    for k in range(1, n):
        pos_copy(me, (me + k) % n).wait_send()

    for d in range(1, rim + 1):
        @pl.when(me - d >= 0)
        def _():
            grad_copy(1, d, sib).wait_send()
            grad_copy(0, d, sib).wait_send()

        @pl.when(me + d < n)
        def _():
            grad_copy(1, d, sib).wait_recv()
            grad_copy(0, d, sib).wait_recv()
            dk_ref[...] += gk_recv[d].astype(F32)
            dv_ref[...] += gv_recv[d].astype(F32)


def local(query, self_keys, self_values, cache_keys, cache_values, cache_pos, d_out):
    n = lax.axis_size("seq")
    rows = query.shape[0]
    cached = cache_keys.shape[0]
    rim = (WINDOW + rows - 2) // rows
    stacked = GROUP * rows
    vmem = pl.BlockSpec(memory_space=pltpu.VMEM)
    att, dq, dk, dv = pl.pallas_call(
        functools.partial(kernel, n),
        out_shape=(
            jax.ShapeDtypeStruct((rows, GROUP * HD), BF16),
            jax.ShapeDtypeStruct((rows, GROUP * HD), BF16),
            jax.ShapeDtypeStruct((rows, HD), F32),
            jax.ShapeDtypeStruct((rows, HD), F32),
        ),
        in_specs=[vmem] * 7,
        out_specs=(vmem,) * 4,
        scratch_shapes=[
            pltpu.VMEM((stacked, HD), BF16),
            pltpu.VMEM((stacked, HD), BF16),
            pltpu.VMEM((n, cached + rows, HD), BF16),
            pltpu.VMEM((n, cached + rows, HD), BF16),
            pltpu.VMEM((n, 1, cached), jnp.int32),
            pltpu.VMEM((n, stacked, cached), F32),
            pltpu.VMEM((n, stacked, cached), F32),
            pltpu.VMEM((rim + 1, stacked, rows), F32),
            pltpu.VMEM((stacked, 128), F32),
            pltpu.VMEM((stacked, 128), F32),
            pltpu.VMEM((stacked, HD), F32),
            pltpu.VMEM((rim + 1, rows, HD), BF16),
            pltpu.VMEM((rim + 1, rows, HD), BF16),
            pltpu.VMEM((rim + 1, rows, HD), BF16),
            pltpu.VMEM((rim + 1, rows, HD), BF16),
            pltpu.SemaphoreType.DMA((2, 3, n)),
            pltpu.SemaphoreType.DMA((2, n)),
            pltpu.SemaphoreType.DMA((n,)),
            pltpu.SemaphoreType.DMA((n,)),
            pltpu.SemaphoreType.DMA((2, rim + 1)),
            pltpu.SemaphoreType.DMA((2, rim + 1)),
        ],
        compiler_params=pltpu.CompilerParams(
            collective_id=0, has_side_effects=True, vmem_limit_bytes=56 * 2**20
        ),
    )(
        query, self_keys, self_values, cache_keys, cache_values,
        cache_pos.reshape(1, cached), d_out,
    )
    return att, dq, (dk * HD ** -0.5).astype(BF16), dv.astype(BF16)


def solution(mesh):
    split = P(("batch", "seq"), "kvh")
    return jax.shard_map(
        local,
        mesh=mesh,
        in_specs=(split, split, split, split, split, P(("batch", "seq")), split),
        out_specs=(split, split, split, split),
        check_vma=False,
    )
```

time: 136 us -> 51.4 us (0.38)
  the two profiles are of different devices: /device:TPU:19 before, /device:TPU:7 now
where the time goes in v1:
time: 51.4 us; the launch traced here: 51.1 us
  Pallas kernels  45.9 us (89%)
  other arithmetic  2.96 us (6%)
  local copies, waits for them, and re-layouts  1.65 us (3%)
  between operations  0.65 us (1%)
    pallas_call x1, Pallas kernels, local(): pl.pallas_call(functools.partial(kernel, n), out_shape=(jax.ShapeDtypeStr...  45.9 us
    convert_element_type x2, other arithmetic, local(): return (att, dq, (dk * HD ** (-0.5)).astype(BF16), dv.astype(BF16))  2.96 us
    unnamed x6, local copies, waits for them, and re-layouts  1.65 us

profile of v1, /device:TPU:7, one launch (start us, length us, event | category | flops | bytes accessed | tf_op | source)
XLA Modules:
  0.0 51.1 jit_solution(11867810313905323688)
XLA Ops:
  0.6 45.9 %shard_map.102 = (bf16[128,640]{1,0:T(8,128)(2,1)}, bf16[128,640]{1,0:T(8,128)(2,1)}, f32[128,128]{1,0:T(8,128)}, f32[128,128]{1,0:T(8,128)}) custom-call(bf16[128,640]{1,0:T(8,128)(2,1)} %q_ref.1, bf16[128,128]{1,0:T(8,128)(2,1)} %sk_ref.1, bf16[128,128]{1,0:T(8,128)(2,1)} %sv_ref.1, bf16[512,128]{1,0:T(8,128)(2,1)} %ck_ref.1, bf16[512,128]{1,0:T(8,128)(2,1)} %cv_ref.1, ...), custom_call_target="tpu_custom_call" | custom-call | tf_op jit(solution)/shard_map/pallas_call | solution.py:371
  46.5 0.0 copy-start.1
  46.5 1.5 %multiply_convert_fusion = bf16[128,128]{1,0:T(8,128)(2,1)} fusion(f32[128,128]{1,0:T(8,128)} %get-tuple-element.10), kind=kLoop, calls=%fused_computation | loop fusion | flops 32768 | bytes 98304 | tf_op jit(solution)/shard_map/convert_element_type | solution.py:411
  48.0 1.5 %convert_element_type.7 = bf16[128,128]{1,0:T(8,128)(2,1)} convert(f32[128,128]{1,0:T(8,128)} %get-tuple-element.11) | non-fusion elementwise | flops 16384 | bytes 98304 | tf_op jit(solution)/shard_map/convert_element_type | solution.py:411
  49.5 0.0 copy-done.1
  49.5 0.0 copy-start
  49.5 0.7 %copy.13 = bf16[128,640]{1,0:T(8,128)(2,1)} copy(bf16[128,640]{1,0:T(8,128)(2,1)S(1)} %copy-done.1) | data formatting | bytes 327680
  50.2 0.3 copy-done
  50.5 0.7 %copy.14 = bf16[128,640]{1,0:T(8,128)(2,1)} copy(bf16[128,640]{1,0:T(8,128)(2,1)S(1)} %copy-done) | data formatting | bytes 327680
Async XLA Ops:
  46.5 3.0 %copy-start.1 = (bf16[128,640]{1,0:T(8,128)(2,1)S(1)}, bf16[128,640]{1,0:T(8,128)(2,1)}, u32[]{:S(2)}) copy-start(bf16[128,640]{1,0:T(8,128)(2,1)} %get-tuple-element.16) | copy-start | bytes 491524
  49.5 1.0 %copy-start = (bf16[128,640]{1,0:T(8,128)(2,1)S(1)}, bf16[128,640]{1,0:T(8,128)(2,1)}, u32[]{:S(2)}) copy-start(bf16[128,640]{1,0:T(8,128)(2,1)} %get-tuple-element.17) | copy-start | bytes 491524

commit v2 on v1

--- a/solution.py
+++ b/solution.py
@@ -40,7 +40,7 @@
 def kernel(
     n, q_ref, sk_ref, sv_ref, ck_ref, cv_ref, cp_ref, do_ref,
     att_ref, dq_ref, dk_ref, dv_ref,
-    qs, ds_out, kbuf, vbuf, pos, s_ref, dp_ref, sw_ref, m_ref, l_ref, acc,
+    qs, ds_out, kbuf, vbuf, pos, s_ref, dp_ref, sw_ref, dw_ref, m_ref, l_ref, acc, own_k, own_v,
     gk_send, gv_send, gk_recv, gv_recv,
     send_sem, recv_sem, pos_send, pos_recv, g_send, g_recv,
 ):
@@ -198,33 +198,46 @@
             s_ref[o, head(g)] = s
             m_ref[head(g)] = jnp.maximum(m_ref[head(g)], lane_tiles(s, jnp.maximum))
 
+    first = jnp.maximum(me - rim, 0)
+    near_end = min(rim_chips, chips - 1)
+    delta_index = lax.broadcasted_iota(jnp.int32, (rows, rows), 0) - lax.broadcasted_iota(
+        jnp.int32, (rows, rows), 1
+    )
+
+    def window_scores():
+        @pl.loop(first, me + 1)
+        def _(o):
+            d = me - o
+            gap = delta_index + d * rows
+            vis = (gap >= 0) & (gap < WINDOW)
+            s = dot_nt(qs[...], kbuf[o, cached:])
+            s = jnp.concatenate([jnp.where(vis, s[head(g)], NEG) for g in range(GROUP)], axis=0)
+            sw_ref[d] = s
+            m_ref[...] = jnp.maximum(m_ref[...], s)
+
+    def window_values():
+        @pl.loop(first, me + 1)
+        def _(o):
+            d = me - o
+            v = vbuf[o, cached:]
+            acc[...] += dot_nn(sw_ref[d].astype(BF16), v)
+            dw_ref[d] = dot_nt(ds_out[...], v)
+
     @pl.loop(0, chips)
     def _(t):
         @pl.when(t > 0)
         def _():
             relay(0, t, "go")
 
-        @pl.when(t == 1)
-        def _():
-            relay(1, 0, "go")
-
         consume(0, t, score_shard)
 
-    first = jnp.maximum(me - rim, 0)
-    delta_index = lax.broadcasted_iota(jnp.int32, (rows, rows), 0) - lax.broadcasted_iota(
-        jnp.int32, (rows, rows), 1
-    )
-
-    @pl.loop(first, me + 1)
-    def _(o):
-        d = me - o
-        gap = delta_index + d * rows
-        vis = (gap >= 0) & (gap < WINDOW)
-        for g in range(GROUP):
-            s = dot_nt(qs[head(g)], kbuf[o, cached:])
-            s = jnp.where(vis, s, NEG)
-            sw_ref[d, head(g)] = s
-            m_ref[head(g)] = jnp.maximum(m_ref[head(g)], s)
+        @pl.when(t > 0)
+        def _():
+            relay(1, t - 1, "go")
+
+        @pl.when(t == near_end)
+        def _():
+            window_scores()
 
     for g in range(GROUP):
         top = jnp.max(m_ref[head(g)], axis=1, keepdims=True)
@@ -240,10 +253,9 @@
     @pl.loop(first, me + 1)
     def _(o):
         d = me - o
-        for g in range(GROUP):
-            p = jnp.exp2((sw_ref[d, head(g)] - m_ref[head(g)]) * scale2)
-            sw_ref[d, head(g)] = p
-            l_ref[head(g)] += p
+        p = jnp.exp2((sw_ref[d] - m_ref[...]) * scale2)
+        sw_ref[d] = p
+        l_ref[...] += p
 
     for g in range(GROUP):
         total = jnp.sum(l_ref[head(g)], axis=1, keepdims=True)
@@ -263,16 +275,14 @@
     @pl.loop(first, me + 1)
     def _(o):
         d = me - o
-        total = jnp.zeros((rows, HD), F32)
-        for g in range(GROUP):
-            w = sw_ref[d, head(g)] * l_ref[head(g)]
-            sw_ref[d, head(g)] = w
-            total = total + dot_tn(w.astype(BF16), ds_out[head(g)])
+        w = sw_ref[d] * l_ref[...]
+        sw_ref[d] = w
+        total = dot_tn(w.astype(BF16), ds_out[...])
         gv_send[d] = total.astype(BF16)
 
         @pl.when(d == 0)
         def _():
-            dv_ref[...] = total
+            own_v[...] = total
 
         @pl.when(d > 0)
         def _():
@@ -287,18 +297,15 @@
 
     @pl.loop(0, chips)
     def _(t):
-        @pl.when(t > 0)
+        @pl.when(t == chips - 1)
         def _():
             relay(1, t, "go")
 
         consume(1, t, value_shard)
 
-    @pl.loop(first, me + 1)
-    def _(o):
-        d = me - o
-        v = vbuf[o, cached:]
-        for g in range(GROUP):
-            acc[head(g)] += dot_nn(sw_ref[d, head(g)].astype(BF16), v)
+        @pl.when(t == near_end)
+        def _():
+            window_values()
 
     for g in range(GROUP):
         out = acc[head(g)].astype(BF16)
@@ -310,19 +317,14 @@
     @pl.loop(first, me + 1)
     def _(o):
         d = me - o
-        v = vbuf[o, cached:]
-        key = kbuf[o, cached:]
-        total = jnp.zeros((rows, HD), F32)
-        for g in range(GROUP):
-            dp = dot_nt(ds_out[head(g)], v)
-            gs = (sw_ref[d, head(g)] * (dp - m_ref[head(g)])).astype(BF16)
-            total = total + dot_tn(gs, qs[head(g)])
-            acc[head(g)] += dot_nn(gs, key)
+        gs = (sw_ref[d] * (dw_ref[d] - m_ref[...])).astype(BF16)
+        total = dot_tn(gs, qs[...])
+        acc[...] += dot_nn(gs, kbuf[o, cached:])
         gk_send[d] = total.astype(BF16)
 
         @pl.when(d == 0)
         def _():
-            dk_ref[...] = total
+            own_k[...] = total
 
         @pl.when(d > 0)
         def _():
@@ -357,8 +359,23 @@
         def _():
             grad_copy(1, d, sib).wait_recv()
             grad_copy(0, d, sib).wait_recv()
-            dk_ref[...] += gk_recv[d].astype(F32)
-            dv_ref[...] += gv_recv[d].astype(F32)
+            own_k[...] += gk_recv[d].astype(F32)
+            own_v[...] += gv_recv[d].astype(F32)
+
+    dk_ref[...] = (own_k[...] * scale).astype(BF16)
+    dv_ref[...] = own_v[...].astype(BF16)
+
+
+def hand_over(*refs):
+    count = len(refs) // 2
+    sems = refs[-1]
+    copies = [
+        pltpu.make_async_copy(refs[i], refs[count + i], sems.at[i]) for i in range(count)
+    ]
+    for copy in copies:
+        copy.start()
+    for copy in copies:
+        copy.wait()
 
 
 def local(query, self_keys, self_values, cache_keys, cache_values, cache_pos, d_out):
@@ -368,13 +385,13 @@
     rim = (WINDOW + rows - 2) // rows
     stacked = GROUP * rows
     vmem = pl.BlockSpec(memory_space=pltpu.VMEM)
-    att, dq, dk, dv = pl.pallas_call(
+    results = pl.pallas_call(
         functools.partial(kernel, n),
         out_shape=(
             jax.ShapeDtypeStruct((rows, GROUP * HD), BF16),
             jax.ShapeDtypeStruct((rows, GROUP * HD), BF16),
-            jax.ShapeDtypeStruct((rows, HD), F32),
-            jax.ShapeDtypeStruct((rows, HD), F32),
+            jax.ShapeDtypeStruct((rows, HD), BF16),
+            jax.ShapeDtypeStruct((rows, HD), BF16),
         ),
         in_specs=[vmem] * 7,
         out_specs=(vmem,) * 4,
@@ -387,9 +404,12 @@
             pltpu.VMEM((n, stacked, cached), F32),
             pltpu.VMEM((n, stacked, cached), F32),
             pltpu.VMEM((rim + 1, stacked, rows), F32),
+            pltpu.VMEM((rim + 1, stacked, rows), F32),
             pltpu.VMEM((stacked, 128), F32),
             pltpu.VMEM((stacked, 128), F32),
             pltpu.VMEM((stacked, HD), F32),
+            pltpu.VMEM((rows, HD), F32),
+            pltpu.VMEM((rows, HD), F32),
             pltpu.VMEM((rim + 1, rows, HD), BF16),
             pltpu.VMEM((rim + 1, rows, HD), BF16),
             pltpu.VMEM((rim + 1, rows, HD), BF16),
@@ -408,7 +428,14 @@
         query, self_keys, self_values, cache_keys, cache_values,
         cache_pos.reshape(1, cached), d_out,
     )
-    return att, dq, (dk * HD ** -0.5).astype(BF16), dv.astype(BF16)
+    anywhere = pl.BlockSpec(memory_space=pl.ANY)
+    return pl.pallas_call(
+        hand_over,
+        out_shape=tuple(jax.ShapeDtypeStruct(x.shape, x.dtype) for x in results),
+        in_specs=[anywhere] * len(results),
+        out_specs=(anywhere,) * len(results),
+        scratch_shapes=[pltpu.SemaphoreType.DMA((len(results),))],
+    )(*results)
 
 
 def solution(mesh):

time: 51.4 us -> 55.1 us (1.072)
  the two profiles are of different devices: /device:TPU:7 before, /device:TPU:19 now
where the time goes in v2:
time: 55.1 us; the launch traced here: 55 us
  Pallas kernels  54.3 us (99%)
  between operations  0.64 us (1%)
    pallas_call x1, Pallas kernels, local(): pl.pallas_call(functools.partial(kernel, n), out_shape=(jax.ShapeDtypeStr...  41.3 us
    pallas_call x1, Pallas kernels, local(): pl.pallas_call(hand_over, out_shape=tuple((jax.ShapeDtypeStruct(x.shape,...  13.1 us

profile of v2, /device:TPU:19, one launch (start us, length us, event | category | flops | bytes accessed | tf_op | source)
XLA Modules:
  0.0 55.0 jit_solution(13086538635564282367)
XLA Ops:
  0.6 41.3 %shard_map.102 = (bf16[128,640]{1,0:T(8,128)(2,1)}, bf16[128,640]{1,0:T(8,128)(2,1)}, bf16[128,128]{1,0:T(8,128)(2,1)}, bf16[128,128]{1,0:T(8,128)(2,1)}) custom-call(bf16[128,640]{1,0:T(8,128)(2,1)} %q_ref.1, bf16[128,128]{1,0:T(8,128)(2,1)} %sk_ref.1, bf16[128,128]{1,0:T(8,128)(2,1)} %sv_ref.1, bf16[512,128]{1,0:T(8,128)(2,1)} %ck_ref.1, ...), custom_call_target="tpu_custom_call" | custom-call | tf_op jit(solution)/shard_map/pallas_call | solution.py:388
  41.9 13.1 %shard_map.103 = (bf16[128,640]{1,0:T(8,128)(2,1)}, bf16[128,640]{1,0:T(8,128)(2,1)}, bf16[128,128]{1,0:T(8,128)(2,1)}, bf16[128,128]{1,0:T(8,128)(2,1)}) custom-call(bf16[128,640]{1,0:T(8,128)(2,1)} %get-tuple-element.8.refs_0_, bf16[128,640]{1,0:T(8,128)(2,1)} %get-tuple-element.9.refs_1_, bf16[128,128]{1,0:T(8,128)(2,1)} %get-tuple-element.10.refs_2_, ...), custom_call_target="tpu_custom_call" | custom-call | tf_op jit(solution)/shard_map/pallas_call | solution.py:432

commit v3 on v2

--- a/solution.py
+++ b/solution.py
@@ -170,6 +170,7 @@
         )
 
     relay(0, 0, "go")
+    relay(1, 0, "go")
     for k in range(1, n):
         pos_copy(me, (me + k) % n).start()
 
@@ -233,7 +234,7 @@
 
         @pl.when(t > 0)
         def _():
-            relay(1, t - 1, "go")
+            relay(1, t, "go")
 
         @pl.when(t == near_end)
         def _():
@@ -297,10 +298,6 @@
 
     @pl.loop(0, chips)
     def _(t):
-        @pl.when(t == chips - 1)
-        def _():
-            relay(1, t, "go")
-
         consume(1, t, value_shard)
 
         @pl.when(t == near_end)
@@ -368,14 +365,8 @@
 
 def hand_over(*refs):
     count = len(refs) // 2
-    sems = refs[-1]
-    copies = [
-        pltpu.make_async_copy(refs[i], refs[count + i], sems.at[i]) for i in range(count)
-    ]
-    for copy in copies:
-        copy.start()
-    for copy in copies:
-        copy.wait()
+    for i in range(count):
+        refs[count + i][...] = refs[i][...]
 
 
 def local(query, self_keys, self_values, cache_keys, cache_values, cache_pos, d_out):
@@ -428,13 +419,11 @@
         query, self_keys, self_values, cache_keys, cache_values,
         cache_pos.reshape(1, cached), d_out,
     )
-    anywhere = pl.BlockSpec(memory_space=pl.ANY)
     return pl.pallas_call(
         hand_over,
         out_shape=tuple(jax.ShapeDtypeStruct(x.shape, x.dtype) for x in results),
-        in_specs=[anywhere] * len(results),
-        out_specs=(anywhere,) * len(results),
-        scratch_shapes=[pltpu.SemaphoreType.DMA((len(results),))],
+        in_specs=[vmem] * len(results),
+        out_specs=(vmem,) * len(results),
     )(*results)
 
 

time: 55.1 us -> 43.6 us (0.79)
  Pallas kernels: 54.3 us -> 42.4 us
    pallas_call x1, Pallas kernels: 13.1 us -> 1.75 us  [local(): pl.pallas_call(hand_over, out_shape=tuple((jax.ShapeDtypeStruct(x.shape,...]
    pallas_call x1, Pallas kernels: 41.3 us -> 40.7 us  [local(): pl.pallas_call(functools.partial(kernel, n), out_shape=(jax.ShapeDtypeStr...]
where the time goes in v3:
time: 43.6 us; the launch traced here: 43.1 us
  Pallas kernels  42.4 us (97%)
  between operations  0.64 us (1%)
    pallas_call x1, Pallas kernels, local(): pl.pallas_call(functools.partial(kernel, n), out_shape=(jax.ShapeDtypeStr...  40.7 us
    pallas_call x1, Pallas kernels, local(): pl.pallas_call(hand_over, out_shape=tuple((jax.ShapeDtypeStruct(x.shape,...  1.75 us

profile of v3, /device:TPU:19, one launch (start us, length us, event | category | flops | bytes accessed | tf_op | source)
XLA Modules:
  0.0 43.1 jit_solution(16522035840353922141)
XLA Ops:
  0.6 40.7 %shard_map.102 = (bf16[128,640]{1,0:T(8,128)(2,1)}, bf16[128,640]{1,0:T(8,128)(2,1)}, bf16[128,128]{1,0:T(8,128)(2,1)}, bf16[128,128]{1,0:T(8,128)(2,1)}) custom-call(bf16[128,640]{1,0:T(8,128)(2,1)} %q_ref.1, bf16[128,128]{1,0:T(8,128)(2,1)} %sk_ref.1, bf16[128,128]{1,0:T(8,128)(2,1)} %sv_ref.1, bf16[512,128]{1,0:T(8,128)(2,1)} %ck_ref.1, ...), custom_call_target="tpu_custom_call" | custom-call | tf_op jit(solution)/shard_map/pallas_call | solution.py:379
  41.3 1.8 %shard_map.103 = (bf16[128,640]{1,0:T(8,128)(2,1)}, bf16[128,640]{1,0:T(8,128)(2,1)}, bf16[128,128]{1,0:T(8,128)(2,1)}, bf16[128,128]{1,0:T(8,128)(2,1)}) custom-call(bf16[128,640]{1,0:T(8,128)(2,1)} %get-tuple-element.8.refs_0_, bf16[128,640]{1,0:T(8,128)(2,1)} %get-tuple-element.9.refs_1_, bf16[128,128]{1,0:T(8,128)(2,1)} %get-tuple-element.10.refs_2_, ...), custom_call_target="tpu_custom_call" | custom-call | tf_op jit(solution)/shard_map/pallas_call | solution.py:422

commit v4 on v3

--- a/solution.py
+++ b/solution.py
@@ -232,7 +232,7 @@
 
         consume(0, t, score_shard)
 
-        @pl.when(t > 0)
+        @pl.when((t > 0) & (t < chips - 1))
         def _():
             relay(1, t, "go")
 
@@ -298,6 +298,10 @@
 
     @pl.loop(0, chips)
     def _(t):
+        @pl.when(t == chips - 1)
+        def _():
+            relay(1, t, "go")
+
         consume(1, t, value_shard)
 
         @pl.when(t == near_end)

time: 43.6 us -> 43.6 us (level)
  no operation moved by 1% of the time
where the time goes in v4:
time: 43.6 us; the launch traced here: 43.1 us
  Pallas kernels  42.5 us (97%)
  between operations  0.64 us (1%)
    pallas_call x1, Pallas kernels, local(): pl.pallas_call(functools.partial(kernel, n), out_shape=(jax.ShapeDtypeStr...  40.7 us
    pallas_call x1, Pallas kernels, local(): pl.pallas_call(hand_over, out_shape=tuple((jax.ShapeDtypeStruct(x.shape,...  1.75 us

profile of v4, /device:TPU:19, one launch (start us, length us, event | category | flops | bytes accessed | tf_op | source)
XLA Modules:
  0.0 43.1 jit_solution(9688976713317158155)
XLA Ops:
  0.6 40.7 %shard_map.102 = (bf16[128,640]{1,0:T(8,128)(2,1)}, bf16[128,640]{1,0:T(8,128)(2,1)}, bf16[128,128]{1,0:T(8,128)(2,1)}, bf16[128,128]{1,0:T(8,128)(2,1)}) custom-call(bf16[128,640]{1,0:T(8,128)(2,1)} %q_ref.1, bf16[128,128]{1,0:T(8,128)(2,1)} %sk_ref.1, bf16[128,128]{1,0:T(8,128)(2,1)} %sv_ref.1, bf16[512,128]{1,0:T(8,128)(2,1)} %ck_ref.1, ...), custom_call_target="tpu_custom_call" | custom-call | tf_op jit(solution)/shard_map/pallas_call | solution.py:383
  41.4 1.8 %shard_map.103 = (bf16[128,640]{1,0:T(8,128)(2,1)}, bf16[128,640]{1,0:T(8,128)(2,1)}, bf16[128,128]{1,0:T(8,128)(2,1)}, bf16[128,128]{1,0:T(8,128)(2,1)}) custom-call(bf16[128,640]{1,0:T(8,128)(2,1)} %get-tuple-element.8.refs_0_, bf16[128,640]{1,0:T(8,128)(2,1)} %get-tuple-element.9.refs_1_, bf16[128,128]{1,0:T(8,128)(2,1)} %get-tuple-element.10.refs_2_, ...), custom_call_target="tpu_custom_call" | custom-call | tf_op jit(solution)/shard_map/pallas_call | solution.py:426
